TPU v7x, 32 devices: a whole 2x2x4 slice. The times are simulated.
32 devices in a mesh: gx: 8 (over y, x, core), gy: 4 (over z).
Axes of the slice: x: 2, y: 2, z: 4, core: 2. Of those that a mesh axis runs over, the one named last changes fastest.
Arguments:
- east_blocks: int32 [16, 4], P(None, 'gy'), may hold values from 0 to 2, as said below
- job_code: int32 [200, 4], P('gx', 'gy'), may hold values from -1 to 554, as said below
- factor_panels: bfloat16 [200, 4, 2, 1536, 128], P('gx', 'gy'), as said below
- dual_rhs: float32 [16, 4, 256, 384], P('gx', 'gy'), may hold values from -6 to 6
Outputs:
- multipliers: float32 [16, 4, 256, 384], P('gx', 'gy')
- residual: float32 [16, 4, 256, 384], P('gx', 'gy')
Inputs may be any that keep to these rules, and one draw needn't show every extreme that they name: `east_blocks`: in each row sy the faces sx = s0 to s0 + 3 carry 2 blocks, for a start s0 drawn per row from 1 to 10; the other faces carry 1, and the face at sx = 15 carries 0. `job_code`: A code (sx * 6 + bi) * 6 + bj names the upper tile bi <= bj < nb of subdomain (sx, sy) for column sy. In each column the live tiles, ordered by sx, then bi, then bj, are numbered k = 0, 1, ... and sit at row (k % 8) * 25 + k // 8; all other slots hold -1. Hence one device of gx forms at most 6 tiles of the subdomains of one gx index, and exactly 6 for some. `factor_panels`: A live slot holds column blocks bi and bj of subdomain (sx, sy)'s factor of 1536 rows and 768 columns, the same block wherever it appears; empty slots hold zeros.
All inputs are finite; a program needn't handle non-finite values.
Results may differ from a plain program's by a relative error of at most 0.0059.
Values may be sent and summed in bfloat16 or wider, within the bound.
A program may use at most 128 MiB of HBM per device.

v0:
```python
import jax
import jax.numpy as jnp
from jax import lax
from jax.sharding import PartitionSpec as P

NB = 6
ITERS = 4


CHEB_LOW = 0.2
CHEB_HIGH = 7.0


def from_behind(value, axis, steps):
    count = lax.axis_size(axis)
    initial, last = (max(0, -steps), min(count, count - steps))
    return lax.ppermute(value, axis, [(source, source + steps) for source in range(initial, last)])


def tile_form(upper_tiles):
    upper_f = upper_tiles.astype(jnp.float32)
    flipped = jnp.swapaxes(jnp.swapaxes(upper_f, 1, 2), 3, 4)
    block_row = jnp.arange(NB, dtype=jnp.int32)
    keep_upper = (block_row[:, None] <= block_row[None, :])[None, :, :, None, None]
    return jnp.where(keep_upper, upper_f, flipped)


def slot_sources(count_row):
    west_n = count_row[0]
    east_n = count_row[1]
    south_n = count_row[2]
    north_n = count_row[3]
    within = jnp.array([0, 1, 0, 1, 0, 0], jnp.int32)
    offsets = jnp.stack(
        [0 * west_n, 0 * west_n, west_n, west_n, west_n + east_n, west_n + east_n + south_n]
    )
    limits = jnp.stack([west_n, west_n, east_n, east_n, south_n, north_n])
    source = jnp.minimum(offsets + within, NB - 1)
    alive = (within < limits).astype(jnp.float32)
    return (source, alive)


def arranged(full_tiles, count_row):
    source, alive = slot_sources(count_row)
    picked = jnp.take(jnp.take(full_tiles, source, axis=0), source, axis=1)
    picked = picked * (alive[:, None] * alive[None, :])[:, :, None, None]
    block_len = full_tiles.shape[-1]
    return picked.transpose(0, 2, 1, 3).reshape(NB * block_len, NB * block_len)


def face_mask(counts, block_len):
    east_lane = jnp.arange(2 * block_len, dtype=jnp.int32) // block_len
    east_ok = east_lane < counts[..., 1:2]
    north_ok = jnp.zeros((block_len,), jnp.int32) < counts[..., 3:4]
    return jnp.concatenate([east_ok, north_ok], axis=-1).astype(jnp.float32)


def shards(east_blocks, job_code, factor_panels, dual_rhs):
    gx_count = lax.axis_size("gx")
    gy_count = lax.axis_size("gy")
    gx_index = lax.axis_index("gx")
    gy_index = lax.axis_index("gy")
    block_len = factor_panels.shape[-1]
    sub_count = dual_rhs.shape[0]
    column = east_blocks[:, 0]
    west_column = jnp.concatenate([jnp.zeros((1,), jnp.int32), column[:-1]])
    first_sub = gx_index * sub_count
    east_own = lax.dynamic_slice_in_dim(column, first_sub, sub_count)
    west_own = lax.dynamic_slice_in_dim(west_column, first_sub, sub_count)
    south_own = jnp.broadcast_to((gy_index > 0).astype(jnp.int32), (sub_count,))
    north_own = jnp.broadcast_to((gy_index < gy_count - 1).astype(jnp.int32), (sub_count,))
    counts = jnp.stack([west_own, east_own, south_own, north_own], axis=-1)
    tiles = jnp.einsum(
        "jka,jkb->jab",
        factor_panels[:, 0, 0],
        factor_panels[:, 0, 1],
        preferred_element_type=jnp.float32,
    ).astype(jnp.bfloat16)
    tile_codes = job_code[:, 0]
    job_count = tile_codes.shape[0]
    is_valid = tile_codes >= 0
    owner_gx = jnp.where(is_valid, tile_codes // (NB * NB) // sub_count, 0)
    slot_cap = (sub_count * NB * (NB + 1) // 2 + gx_count - 1) // gx_count
    job_order = jnp.arange(job_count, dtype=jnp.int32)
    same_owner = (
        (owner_gx[:, None] == owner_gx[None, :])
        & is_valid[None, :]
        & (job_order[None, :] < job_order[:, None])
    )
    slot_rank = jnp.sum(same_owner.astype(jnp.int32), axis=1)
    send_slot = jnp.where(is_valid, owner_gx * slot_cap + slot_rank, gx_count * slot_cap)
    send_tiles = (
        jnp.zeros((gx_count * slot_cap, block_len, block_len), jnp.bfloat16)
        .at[send_slot]
        .set(tiles, mode="drop")
    )
    send_tiles = send_tiles.reshape(gx_count, slot_cap, block_len, block_len)
    send_codes = (
        jnp.full((gx_count * slot_cap,), -1, jnp.int32).at[send_slot].set(tile_codes, mode="drop")
    )
    send_codes = send_codes.reshape(gx_count, slot_cap)
    got_tiles, got_codes = (
        lax.all_to_all(send_tiles, "gx", split_axis=0, concat_axis=0, tiled=True),
        lax.all_to_all(send_codes, "gx", split_axis=0, concat_axis=0, tiled=True),
    )
    flat_codes = got_codes.reshape(-1)
    flat_tiles = got_tiles.reshape(-1, block_len, block_len)
    local_index = jnp.where(
        flat_codes >= 0,
        flat_codes // (NB * NB) % sub_count * (NB * NB) + flat_codes % (NB * NB),
        sub_count * NB * NB,
    )
    upper_tiles = (
        jnp.zeros((sub_count * NB * NB, block_len, block_len), jnp.bfloat16)
        .at[local_index]
        .set(flat_tiles, mode="drop")
    )
    full_tiles = tile_form(upper_tiles.reshape(sub_count, NB, NB, block_len, block_len))
    matrices = jax.vmap(arranged)(full_tiles, counts)
    residual = dual_rhs[:, 0] * face_mask(counts, block_len)[:, None, :]
    cheb_center = (CHEB_HIGH + CHEB_LOW) / 2.0
    cheb_radius = (CHEB_HIGH - CHEB_LOW) / 2.0
    cheb_ratio = cheb_center / cheb_radius
    cheb_rho = 1.0 / cheb_ratio
    update = residual / cheb_center
    multipliers = jnp.zeros_like(residual)
    for sweep in range(ITERS):
        multipliers = multipliers + update
        east_part = update[..., : 2 * block_len]
        to_north_part = update[..., 2 * block_len :]
        from_west = from_behind(east_part[sub_count - 1], "gx", 1)
        from_south = from_behind(to_north_part, "gy", 1)
        west_in = -jnp.concatenate([from_west[None], east_part[: sub_count - 1]], axis=0)
        image = jnp.einsum(
            "ncm,nmk->nck",
            jnp.concatenate([west_in, east_part, -from_south, to_north_part], axis=-1),
            matrices,
            precision=lax.Precision.HIGHEST,
        )
        west_part = image[..., : 2 * block_len]
        split_east_part = image[..., 2 * block_len : 4 * block_len]
        south_part = image[..., 4 * block_len : 5 * block_len]
        split_north_part = image[..., 5 * block_len :]
        from_east = from_behind(west_part[0], "gx", -1)
        from_north = from_behind(south_part, "gy", -1)
        east_near = jnp.concatenate([west_part[1:], from_east[None]], axis=0)
        residual = residual - jnp.concatenate(
            [split_east_part - east_near, split_north_part - from_north], axis=-1
        )
        rho_next = 1.0 / (2.0 * cheb_ratio - cheb_rho)
        update = rho_next * cheb_rho * update + 2.0 * rho_next / cheb_radius * residual
        cheb_rho = rho_next
    return (multipliers[:, None], residual[:, None])


def solution(mesh):
    in_specs = (
        P(None, "gy"),
        P("gx", "gy"),
        P("gx", "gy", None, None, None),
        P("gx", "gy", None, None),
    )
    out_specs = (P("gx", "gy", None, None), P("gx", "gy", None, None))
    return jax.shard_map(shards, mesh=mesh, in_specs=in_specs, out_specs=out_specs, check_vma=False)
```

profile of v0, /device:TPU:0, one launch (start us, length us, event | category | flops | bytes accessed | tf_op | source)
XLA Modules:
  0.0 216.2 jit_solution(1389718414493410326)
XLA Ops:
  0.6 0.7 broadcast_compare_fusion.1
  1.3 0.7 fusion.56
  2.0 0.7 fusion.78
  2.6 0.2 convert_reduce_fusion
  2.8 0.7 fusion.57
  3.5 0.8 scatter_custom_fusion
  4.3 0.7 all_to_all.9
  5.0 5.2 %all-to-all-start = ((s32[8,1,6]{2,1,0:T(1,128)}), s32[8,1,6]{2,1,0:T(1,128)S(1)}, u32[]{:S(2)}, u32[]{:S(2)}) async-start(s32[8,1,6]{2,1,0:T(1,128)} %bitcast.14), calls=%async_computation | async-start | bytes 8192 | tf_op jit(solution)/shard_map/all_to_all | solution.py:104
  10.1 0.7 slice_bitcast_fusion.8
  10.9 0.7 add_bitcast_fusion.1
  11.7 1.2 fusion.46
  12.9 0.8 slice_bitcast_fusion.7
  13.7 2.4 %collective-permute-start = (f32[256,256]{1,0:T(8,128)}, f32[256,256]{1,0:T(8,128)S(1)}, u32[]{:S(2)}, u32[]{:S(2)}) collective-permute-start(f32[256,256]{1,0:T(8,128)} %get-tuple-element.36), channel_id=1, source_target_pairs={{0,4},{4,8},{8,12},{12,16},{16,20},{20,24},{24,28},{1,5},{5,9},{9,... | collective-permute-start | bytes 786440 | tf_op jit(solution)/shard_map/ppermute | solution.py:17
  16.2 3.5 %collective-permute-start.1 = (f32[2,256,128]{2,1,0:T(8,128)S(1)}, f32[2,256,128]{2,1,0:T(8,128)S(1)}, u32[]{:S(2)}, u32[]{:S(2)}) collective-permute-start(f32[2,256,128]{2,1,0:T(8,128)S(1)} %slice.187), channel_id=1, source_target_pairs={{0,1},{1,2},{2,3},{4,5},{5,6},{6,7},{8,9},{9,10},{10,11},{12,13},{... | collective-permute-start | bytes 786440 | tf_op jit(solution)/shard_map/ppermute | solution.py:17
  20.0 9.5 %fusion.38 = bf16[25,128,128]{2,1,0:T(8,128)(2,1)S(1)} fusion(bf16[25,1,2,1536,128]{4,3,2,1,0:T(8,128)(2,1)} %param.7), kind=kOutput, calls=%fused_computation.46 | convolution fusion | flops 1258700800 | bytes 20480000 | tf_op jit(solution)/shard_map/jka,jkb->jab/dot_general | solution.py:73
  29.6 0.1 stack.15
  29.7 1.6 broadcast_in_dim.98
  31.3 4.2 %scatter_fusion = bf16[48,128,128]{2,1,0:T(8,128)(2,1)} fusion(bf16[48,128,128]{2,1,0:T(8,128)(2,1)} %broadcast_in_dim.98, s32[25]{0:T(128)S(1)} %fusion.57, bf16[25,128,128]{2,1,0:T(8,128)(2,1)S(1)} %fusion.38), kind=kCustom, calls=%fused_computation.3 | custom fusion | bytes 2457700 | tf_op jit(solution)/shard_map/scatter | solution.py:95
  35.5 3.8 %all-to-all-start.1 = ((bf16[8,6,128,128]{3,2,1,0:T(8,128)(2,1)}), bf16[8,6,128,128]{3,2,1,0:T(8,128)(2,1)S(1)}, u32[]{:S(2)}, u32[]{:S(2)}) async-start(bf16[8,6,128,128]{3,2,1,0:T(8,128)(2,1)} %bitcast.18), calls=%async_computation.1 | async-start | bytes 3145728 | tf_op jit(solution)/shard_map/all_to_all | solution.py:103
  40.3 20.0 %all-to-all-done.1 = bf16[8,6,128,128]{3,2,1,0:T(8,128)(2,1)S(1)} async-done(((bf16[8,6,128,128]{3,2,1,0:T(8,128)(2,1)}), bf16[8,6,128,128]{3,2,1,0:T(8,128)(2,1)S(1)}, u32[]{:S(2)}, u32[]{:S(2)}) %all-to-all-start.1) | async-done | bytes 1572896 | tf_op jit(solution)/shard_map/all_to_all | solution.py:103
  60.4 1.2 copy-done.1
  61.5 0.6 broadcast_in_dim.94
  62.1 5.1 %scatter_fusion.1 = bf16[72,128,128]{2,1,0:T(8,128)(2,1)S(1)} fusion(bf16[72,128,128]{2,1,0:T(8,128)(2,1)S(1)} %broadcast_in_dim.94, s32[48]{0:T(128)S(1)} %fusion.55, bf16[48,128,128]{2,1,0:T(8,128)(2,1)} %bitcast.150), kind=kCustom, calls=%fused_computation.4 | custom fusion | bytes 4718784 | tf_op jit(solution)/shard_map/scatter | solution.py:116
  67.3 3.0 %copy.69 = f32[2,6,6,128,128]{3,4,1,2,0:T(8,128)} copy(bf16[2,6,6,128,128]{4,3,2,1,0:T(8,128)(2,1)S(1)} %bitcast.146) | data formatting | bytes 7077888 | tf_op jit(solution)/shard_map/convert_element_type | solution.py:21
  70.3 5.6 %bitcast_select_fusion = f32[2,6,6,128,128]{4,3,2,1,0:T(8,128)} fusion(f32[2,6,6,128,128]{3,4,1,2,0:T(8,128)} %copy.69, pred[6,6]{1,0:T(8,128)(4,1)S(1)} %iota_compare_fusion.1, bf16[2,6,6,128,128]{4,3,2,1,0:T(8,128)(2,1)S(1)} %bitcast.147), kind=kLoop, calls=%fused_computation.12 | loop fusion | flops 2359296 | bytes 11796516 | tf_op jit(solution)/shard_map/jit(_where)/select_n | solution.py:25
  75.9 5.4 %gather_fusion = f32[12,6,128,128]{3,2,1,0:T(8,128)} fusion(f32[2,6,6,128,128]{4,3,2,1,0:T(8,128)} %bitcast_select_fusion, s32[12]{0:T(128)S(1)} %reshape.246), kind=kCustom, calls=%fused_computation | custom fusion | bytes 9437280 | tf_op jit(solution)/shard_map/vmap(jit(_take))/gather | solution.py:45
  81.3 5.4 %broadcast_select_fusion = f32[2,6,6,128,128]{4,3,2,1,0:T(8,128)} fusion(f32[2,6,6,128,128]{4,3,2,1,0:T(8,128)} %bitcast.148, pred[2,6]{1,0:T(4,128)(4,1)S(1)} %compare_and_fusion), kind=kLoop, calls=%fused_computation.13 | loop fusion | flops 1179648 | bytes 9437196 | tf_op jit(solution)/shard_map/vmap(jit(_take))/select_n | solution.py:45
  86.8 5.4 %gather_fusion.1 = f32[12,6,128,128]{3,2,1,0:T(8,128)} fusion(f32[2,6,6,128,128]{4,3,2,1,0:T(8,128)} %broadcast_select_fusion, s32[12]{0:T(128)S(1)} %reshape.246), kind=kCustom, calls=%fused_computation.1 | custom fusion | bytes 9437280 | tf_op jit(solution)/shard_map/vmap(jit(_take))/gather | solution.py:45
  92.2 2.7 %fusion.5 = f32[2,6,128,6,128]{4,2,1,3,0:T(8,128)S(1)} fusion(f32[2,6,6,128,128]{4,3,2,1,0:T(8,128)} %bitcast.149, f32[2,6,6]{1,2,0:T(8,128)S(1)} %broadcast_multiply_fusion, pred[2,6]{1,0:T(4,128)(4,1)S(1)} %compare_and_fusion), kind=kLoop, calls=%fused_computation.11 | loop fusion | flops 2359296 | bytes 9437484 | tf_op jit(solution)/shard_map/vmap()/mul | solution.py:46
  94.9 5.4 %copy.74 = f32[2,6,128,6,128]{4,3,2,1,0:T(8,128)} copy(f32[2,6,128,6,128]{4,2,1,3,0:T(8,128)S(1)} %fusion.5) | data formatting | bytes 9437184 | tf_op jit(solution)/shard_map/vmap()/mul | solution.py:46
  100.4 6.9 %reshape.244 = f32[2,768,768]{2,1,0:T(8,128)} reshape(f32[2,6,128,6,128]{4,3,2,1,0:T(8,128)} %copy.74) | data formatting | bytes 9437184 | tf_op jit(solution)/shard_map/vmap()/reshape | solution.py:48
  107.3 6.3 %fusion.6 = f32[2,256,768]{2,1,0:T(8,128)S(1)} fusion(f32[2,768,768]{2,1,0:T(8,128)} %reshape.244, f32[2,256,128]{2,1,0:T(8,128)S(1)} %slice.187, f32[2,256,128]{2,1,0:T(8,128)S(1)} %neg.25, f32[2,256,256]{2,1,0:T(8,128)S(1)} %slice-done.2, f32[2,256,256]{2,1,0:T(8,128)S(1)} %maximum_negate_fusion), kind=kOutput, calls=%fused_computation.14 | convolution fusion | flops 3625058304 | bytes 7864320 | tf_op jit(solution)/shard_map/ncm,nmk->nck/dot_general | solution.py:134
  113.7 1.4 collective-permute-start.2
  115.2 1.3 collective-permute-start.3
  116.5 0.8 collective-permute-done.2
  117.4 8.6 %collective-permute-done.3 = f32[2,256,128]{2,1,0:T(8,128)S(1)} collective-permute-done((f32[2,256,128]{2,1,0:T(8,128)S(1)}, f32[2,256,128]{2,1,0:T(8,128)S(1)}, u32[]{:S(2)}, u32[]{:S(2)}) %collective-permute-start.3) | collective-permute-done | bytes 262176 | tf_op jit(solution)/shard_map/ppermute | solution.py:17
  126.0 0.1 multiply_add_fusion.1
  126.2 2.0 collective-permute-start.4
  128.3 4.2 %collective-permute-start.5 = (f32[2,256,128]{2,1,0:T(8,128)S(1)}, f32[2,256,128]{2,1,0:T(8,128)S(1)}, u32[]{:S(2)}, u32[]{:S(2)}) collective-permute-start(f32[2,256,128]{2,1,0:T(8,128)S(1)} %slice.196), channel_id=1, source_target_pairs={{0,1},{1,2},{2,3},{4,5},{5,6},{6,7},{8,9},{9,10},{10,11},{12,13},{... | collective-permute-start | bytes 786440 | tf_op jit(solution)/shard_map/ppermute | solution.py:17
  132.6 6.2 %collective-permute-done.5 = f32[2,256,128]{2,1,0:T(8,128)S(1)} collective-permute-done((f32[2,256,128]{2,1,0:T(8,128)S(1)}, f32[2,256,128]{2,1,0:T(8,128)S(1)}, u32[]{:S(2)}, u32[]{:S(2)}) %collective-permute-start.5) | collective-permute-done | bytes 262176 | tf_op jit(solution)/shard_map/ppermute | solution.py:17
  138.9 4.2 %fusion.14 = f32[2,256,768]{2,1,0:T(8,128)S(1)} fusion(f32[2,768,768]{2,1,0:T(8,128)S(1)} %bitcast.145, f32[2,256,128]{2,1,0:T(8,128)S(1)} %slice.196, f32[2,256,128]{2,1,0:T(8,128)S(1)} %neg.27, f32[2,256,256]{2,1,0:T(8,128)S(1)} %slice.195, f32[2,256,256]{2,1,0:T(8,128)S(1)} %maximum_negate_fusion.1), kind=kOutput, calls=%fused_computation.22 | convolution fusion | flops 3625058304 | bytes 7864320 | tf_op jit(solution)/shard_map/ncm,nmk->nck/dot_general | solution.py:134
  143.1 1.3 collective-permute-start.6
  144.4 1.3 collective-permute-start.7
  145.7 0.8 collective-permute-done.6
  146.6 9.0 %collective-permute-done.7 = f32[2,256,128]{2,1,0:T(8,128)S(1)} collective-permute-done((f32[2,256,128]{2,1,0:T(8,128)S(1)}, f32[2,256,128]{2,1,0:T(8,128)S(1)}, u32[]{:S(2)}, u32[]{:S(2)}) %collective-permute-start.7) | collective-permute-done | bytes 262176 | tf_op jit(solution)/shard_map/ppermute | solution.py:17
  155.6 0.2 multiply_add_fusion
  155.8 2.1 collective-permute-start.8
  158.0 4.1 %collective-permute-start.9 = (f32[2,256,128]{2,1,0:T(8,128)S(1)}, f32[2,256,128]{2,1,0:T(8,128)S(1)}, u32[]{:S(2)}, u32[]{:S(2)}) collective-permute-start(f32[2,256,128]{2,1,0:T(8,128)S(1)} %slice.205), channel_id=1, source_target_pairs={{0,1},{1,2},{2,3},{4,5},{5,6},{6,7},{8,9},{9,10},{10,11},{12,13},{... | collective-permute-start | bytes 786440 | tf_op jit(solution)/shard_map/ppermute | solution.py:17
  162.2 6.1 %collective-permute-done.9 = f32[2,256,128]{2,1,0:T(8,128)S(1)} collective-permute-done((f32[2,256,128]{2,1,0:T(8,128)S(1)}, f32[2,256,128]{2,1,0:T(8,128)S(1)}, u32[]{:S(2)}, u32[]{:S(2)}) %collective-permute-start.9) | collective-permute-done | bytes 262176 | tf_op jit(solution)/shard_map/ppermute | solution.py:17
  168.3 4.2 %fusion.22 = f32[2,256,768]{2,1,0:T(8,128)S(1)} fusion(f32[2,768,768]{2,1,0:T(8,128)S(1)} %bitcast.145, f32[2,256,128]{2,1,0:T(8,128)S(1)} %slice.205, f32[2,256,128]{2,1,0:T(8,128)S(1)} %neg.29, f32[2,256,256]{2,1,0:T(8,128)S(1)} %slice.204, f32[2,256,256]{2,1,0:T(8,128)S(1)} %maximum_negate_fusion.2), kind=kOutput, calls=%fused_computation.30 | convolution fusion | flops 3625058304 | bytes 7864320 | tf_op jit(solution)/shard_map/ncm,nmk->nck/dot_general | solution.py:134
  172.5 1.3 collective-permute-start.10
  173.8 1.3 collective-permute-start.11
  175.1 0.8 collective-permute-done.10
  176.0 9.0 %collective-permute-done.11 = f32[2,256,128]{2,1,0:T(8,128)S(1)} collective-permute-done((f32[2,256,128]{2,1,0:T(8,128)S(1)}, f32[2,256,128]{2,1,0:T(8,128)S(1)}, u32[]{:S(2)}, u32[]{:S(2)}) %collective-permute-start.11) | collective-permute-done | bytes 262176 | tf_op jit(solution)/shard_map/ppermute | solution.py:17
  185.0 0.2 fusion.44
  185.3 2.1 collective-permute-start.12
  187.4 4.3 %collective-permute-start.13 = (f32[2,256,128]{2,1,0:T(8,128)S(1)}, f32[2,256,128]{2,1,0:T(8,128)S(1)}, u32[]{:S(2)}, u32[]{:S(2)}) collective-permute-start(f32[2,256,128]{2,1,0:T(8,128)S(1)} %slice.214), channel_id=1, source_target_pairs={{0,1},{1,2},{2,3},{4,5},{5,6},{6,7},{8,9},{9,10},{10,11},{12,13},{... | collective-permute-start | bytes 786440 | tf_op jit(solution)/shard_map/ppermute | solution.py:17
  191.9 5.8 %collective-permute-done.13 = f32[2,256,128]{2,1,0:T(8,128)S(1)} collective-permute-done((f32[2,256,128]{2,1,0:T(8,128)S(1)}, f32[2,256,128]{2,1,0:T(8,128)S(1)}, u32[]{:S(2)}, u32[]{:S(2)}) %collective-permute-start.13) | collective-permute-done | bytes 262176 | tf_op jit(solution)/shard_map/ppermute | solution.py:17
  197.7 4.2 %fusion.30 = f32[2,256,768]{2,1,0:T(8,128)S(1)} fusion(f32[2,768,768]{2,1,0:T(8,128)S(1)} %bitcast.145, f32[2,256,128]{2,1,0:T(8,128)S(1)} %slice.214, f32[2,256,128]{2,1,0:T(8,128)S(1)} %neg.31, f32[2,256,256]{2,1,0:T(8,128)S(1)} %slice-done.3, f32[2,256,256]{2,1,0:T(8,128)S(1)} %maximum_negate_fusion.3), kind=kOutput, calls=%fused_computation.38 | convolution fusion | flops 3625058304 | bytes 7864320 | tf_op jit(solution)/shard_map/ncm,nmk->nck/dot_general | solution.py:134
  201.9 1.3 collective-permute-start.14
  203.3 1.3 collective-permute-start.15
  204.7 0.7 collective-permute-done.14
  205.4 9.1 %collective-permute-done.15 = f32[2,256,128]{2,1,0:T(8,128)S(1)} collective-permute-done((f32[2,256,128]{2,1,0:T(8,128)S(1)}, f32[2,256,128]{2,1,0:T(8,128)S(1)}, u32[]{:S(2)}, u32[]{:S(2)}) %collective-permute-start.15) | collective-permute-done | bytes 262176 | tf_op jit(solution)/shard_map/ppermute | solution.py:17
  214.6 1.6 fusion.45
  (89 shorter events, 2.8 us)
Async XLA Ops:
  5.0 30.5 %all-to-all-start = ((s32[8,1,6]{2,1,0:T(1,128)}), s32[8,1,6]{2,1,0:T(1,128)S(1)}, u32[]{:S(2)}, u32[]{:S(2)}) async-start(s32[8,1,6]{2,1,0:T(1,128)} %bitcast.14), calls=%async_computation | async-start | bytes 8192 | tf_op jit(solution)/shard_map/all_to_all | solution.py:104
  12.9 26.5 %copy-start.2 = (f32[2,256,384]{2,1,0:T(8,128)}, f32[2,256,384]{2,1,0:T(8,128)S(1)}, u32[]{:S(2)}) copy-start(f32[2,256,384]{2,1,0:T(8,128)S(1)} %fusion.46) | copy-start | bytes 2359300
  13.7 26.5 %collective-permute-start = (f32[256,256]{1,0:T(8,128)}, f32[256,256]{1,0:T(8,128)S(1)}, u32[]{:S(2)}, u32[]{:S(2)}) collective-permute-start(f32[256,256]{1,0:T(8,128)} %get-tuple-element.36), channel_id=1, source_target_pairs={{0,4},{4,8},{8,12},{12,16},{16,20},{20,24},{24,28},{1,5},{5,9},{9,... | collective-permute-start | bytes 786440 | tf_op jit(solution)/shard_map/ppermute | solution.py:17
  16.2 24.1 %collective-permute-start.1 = (f32[2,256,128]{2,1,0:T(8,128)S(1)}, f32[2,256,128]{2,1,0:T(8,128)S(1)}, u32[]{:S(2)}, u32[]{:S(2)}) collective-permute-start(f32[2,256,128]{2,1,0:T(8,128)S(1)} %slice.187), channel_id=1, source_target_pairs={{0,1},{1,2},{2,3},{4,5},{5,6},{6,7},{8,9},{9,10},{10,11},{12,13},{... | collective-permute-start | bytes 786440 | tf_op jit(solution)/shard_map/ppermute | solution.py:17
  20.0 9.7 %copy-start.4 = (s32[6]{0:T(128)S(1)}, s32[6]{0:T(128)}, u32[]{:S(2)}) copy-start(s32[6]{0:T(128)} %constant.137.clone) | copy-start | bytes 76
  35.5 3.8 %copy-start.5 = (s32[16,1]{0,1:T(1,128)S(1)}, s32[16,1]{0,1:T(1,128)}, u32[]{:S(2)}) copy-start(s32[16,1]{0,1:T(1,128)} %param.5) | copy-start | bytes 196
  35.5 24.9 %all-to-all-start.1 = ((bf16[8,6,128,128]{3,2,1,0:T(8,128)(2,1)}), bf16[8,6,128,128]{3,2,1,0:T(8,128)(2,1)S(1)}, u32[]{:S(2)}, u32[]{:S(2)}) async-start(bf16[8,6,128,128]{3,2,1,0:T(8,128)(2,1)} %bitcast.18), calls=%async_computation.1 | async-start | bytes 3145728 | tf_op jit(solution)/shard_map/all_to_all | solution.py:103
  60.4 1.2 copy-start.1
  100.4 6.9 %slice-start.2 = ((f32[2,256,384]{2,1,0:T(8,128)}), f32[2,256,256]{2,1,0:T(8,128)S(1)}, s32[]{:S(2)}) async-start(f32[2,256,384]{2,1,0:T(8,128)} %copy-done.2), calls=%async_computation.4 | async-start | bytes 1048576 | tf_op jit(solution)/shard_map/slice | solution.py:129
  107.3 31.5 %slice-start = ((s8[4718592]{0:T(1024)(128)(4,1)}), s8[4194304]{0:T(1024)(128)(4,1)S(1)}, s32[]{:S(2)}) async-start(s8[4718592]{0:T(1024)(128)(4,1)} %bitcast.144), calls=%async_computation.2 | async-start | bytes 8388608
  113.7 12.3 %copy-start = (f32[2,1,256,384]{3,2,1,0:T(8,128)S(1)}, f32[2,1,256,384]{3,2,1,0:T(8,128)}, u32[]{:S(2)}) copy-start(f32[2,1,256,384]{3,2,1,0:T(8,128)} %param.8) | copy-start | bytes 2359300
  113.7 25.1 %slice-start.1 = ((s8[4718592]{0:T(1024)(128)(4,1)}), s8[524288]{0:T(1024)(128)(4,1)S(1)}, s32[]{:S(2)}) async-start(s8[4718592]{0:T(1024)(128)(4,1)} %bitcast.144), calls=%async_computation.3 | async-start | bytes 1048576
  113.7 3.6 %collective-permute-start.2 = (f32[256,256]{1,0:T(8,128)S(1)}, f32[256,256]{1,0:T(8,128)S(1)}, u32[]{:S(2)}, u32[]{:S(2)}) collective-permute-start(f32[256,256]{1,0:T(8,128)S(1)} %get-tuple-element.29), channel_id=1, source_target_pairs={{4,0},{8,4},{12,8},{16,12},{20,16},{24,20},{28,24},{5,1},{9,5},{13... | collective-permute-start | bytes 786440 | tf_op jit(solution)/shard_map/ppermute | solution.py:17
  115.2 10.8 %collective-permute-start.3 = (f32[2,256,128]{2,1,0:T(8,128)S(1)}, f32[2,256,128]{2,1,0:T(8,128)S(1)}, u32[]{:S(2)}, u32[]{:S(2)}) collective-permute-start(f32[2,256,128]{2,1,0:T(8,128)S(1)} %slice.192), channel_id=1, source_target_pairs={{1,0},{2,1},{3,2},{5,4},{6,5},{7,6},{9,8},{10,9},{11,10},{13,12},{... | collective-permute-start | bytes 786440 | tf_op jit(solution)/shard_map/ppermute | solution.py:17
  126.2 6.4 %collective-permute-start.4 = (f32[256,256]{1,0:T(8,128)S(1)}, f32[256,256]{1,0:T(8,128)S(1)}, u32[]{:S(2)}, u32[]{:S(2)}) collective-permute-start(f32[256,256]{1,0:T(8,128)S(1)} %get-tuple-element.34), channel_id=1, source_target_pairs={{0,4},{4,8},{8,12},{12,16},{16,20},{20,24},{24,28},{1,5},{5,9},{9,... | collective-permute-start | bytes 786440 | tf_op jit(solution)/shard_map/ppermute | solution.py:17
  128.3 10.5 %collective-permute-start.5 = (f32[2,256,128]{2,1,0:T(8,128)S(1)}, f32[2,256,128]{2,1,0:T(8,128)S(1)}, u32[]{:S(2)}, u32[]{:S(2)}) collective-permute-start(f32[2,256,128]{2,1,0:T(8,128)S(1)} %slice.196), channel_id=1, source_target_pairs={{0,1},{1,2},{2,3},{4,5},{5,6},{6,7},{8,9},{9,10},{10,11},{12,13},{... | collective-permute-start | bytes 786440 | tf_op jit(solution)/shard_map/ppermute | solution.py:17
  143.1 3.4 %collective-permute-start.6 = (f32[256,256]{1,0:T(8,128)S(1)}, f32[256,256]{1,0:T(8,128)S(1)}, u32[]{:S(2)}, u32[]{:S(2)}) collective-permute-start(f32[256,256]{1,0:T(8,128)S(1)} %get-tuple-element.27), channel_id=1, source_target_pairs={{4,0},{8,4},{12,8},{16,12},{20,16},{24,20},{28,24},{5,1},{9,5},{13... | collective-permute-start | bytes 786440 | tf_op jit(solution)/shard_map/ppermute | solution.py:17
  144.4 11.2 %collective-permute-start.7 = (f32[2,256,128]{2,1,0:T(8,128)S(1)}, f32[2,256,128]{2,1,0:T(8,128)S(1)}, u32[]{:S(2)}, u32[]{:S(2)}) collective-permute-start(f32[2,256,128]{2,1,0:T(8,128)S(1)} %slice.201), channel_id=1, source_target_pairs={{1,0},{2,1},{3,2},{5,4},{6,5},{7,6},{9,8},{10,9},{11,10},{13,12},{... | collective-permute-start | bytes 786440 | tf_op jit(solution)/shard_map/ppermute | solution.py:17
  155.8 6.3 %collective-permute-start.8 = (f32[256,256]{1,0:T(8,128)S(1)}, f32[256,256]{1,0:T(8,128)S(1)}, u32[]{:S(2)}, u32[]{:S(2)}) collective-permute-start(f32[256,256]{1,0:T(8,128)S(1)} %get-tuple-element.32), channel_id=1, source_target_pairs={{0,4},{4,8},{8,12},{12,16},{16,20},{20,24},{24,28},{1,5},{5,9},{9,... | collective-permute-start | bytes 786440 | tf_op jit(solution)/shard_map/ppermute | solution.py:17
  158.0 10.3 %collective-permute-start.9 = (f32[2,256,128]{2,1,0:T(8,128)S(1)}, f32[2,256,128]{2,1,0:T(8,128)S(1)}, u32[]{:S(2)}, u32[]{:S(2)}) collective-permute-start(f32[2,256,128]{2,1,0:T(8,128)S(1)} %slice.205), channel_id=1, source_target_pairs={{0,1},{1,2},{2,3},{4,5},{5,6},{6,7},{8,9},{9,10},{10,11},{12,13},{... | collective-permute-start | bytes 786440 | tf_op jit(solution)/shard_map/ppermute | solution.py:17
  172.5 3.4 %collective-permute-start.10 = (f32[256,256]{1,0:T(8,128)S(1)}, f32[256,256]{1,0:T(8,128)S(1)}, u32[]{:S(2)}, u32[]{:S(2)}) collective-permute-start(f32[256,256]{1,0:T(8,128)S(1)} %get-tuple-element.25), channel_id=1, source_target_pairs={{4,0},{8,4},{12,8},{16,12},{20,16},{24,20},{28,24},{5,1},{9,5},{13... | collective-permute-start | bytes 786440 | tf_op jit(solution)/shard_map/ppermute | solution.py:17
  173.8 11.2 %collective-permute-start.11 = (f32[2,256,128]{2,1,0:T(8,128)S(1)}, f32[2,256,128]{2,1,0:T(8,128)S(1)}, u32[]{:S(2)}, u32[]{:S(2)}) collective-permute-start(f32[2,256,128]{2,1,0:T(8,128)S(1)} %slice.210), channel_id=1, source_target_pairs={{1,0},{2,1},{3,2},{5,4},{6,5},{7,6},{9,8},{10,9},{11,10},{13,12},{... | collective-permute-start | bytes 786440 | tf_op jit(solution)/shard_map/ppermute | solution.py:17
  185.2 6.6 %copy-start.3 = (f32[2,256,384]{2,1,0:T(8,128)}, f32[2,256,384]{2,1,0:T(8,128)S(1)}, u32[]{:S(2)}) copy-start(f32[2,256,384]{2,1,0:T(8,128)S(1)} %fusion.44) | copy-start | bytes 2359300
  185.3 6.6 %collective-permute-start.12 = (f32[256,256]{1,0:T(8,128)S(1)}, f32[256,256]{1,0:T(8,128)S(1)}, u32[]{:S(2)}, u32[]{:S(2)}) collective-permute-start(f32[256,256]{1,0:T(8,128)S(1)} %get-tuple-element.30), channel_id=1, source_target_pairs={{0,4},{4,8},{8,12},{12,16},{16,20},{20,24},{24,28},{1,5},{5,9},{9,... | collective-permute-start | bytes 786440 | tf_op jit(solution)/shard_map/ppermute | solution.py:17
  187.4 10.3 %collective-permute-start.13 = (f32[2,256,128]{2,1,0:T(8,128)S(1)}, f32[2,256,128]{2,1,0:T(8,128)S(1)}, u32[]{:S(2)}, u32[]{:S(2)}) collective-permute-start(f32[2,256,128]{2,1,0:T(8,128)S(1)} %slice.214), channel_id=1, source_target_pairs={{0,1},{1,2},{2,3},{4,5},{5,6},{6,7},{8,9},{9,10},{10,11},{12,13},{... | collective-permute-start | bytes 786440 | tf_op jit(solution)/shard_map/ppermute | solution.py:17
  191.9 5.9 %slice-start.3 = ((f32[2,256,384]{2,1,0:T(8,128)}), f32[2,256,256]{2,1,0:T(8,128)S(1)}, s32[]{:S(2)}) async-start(f32[2,256,384]{2,1,0:T(8,128)} %copy-done.3), calls=%async_computation.5 | async-start | bytes 1048576 | tf_op jit(solution)/shard_map/slice | solution.py:129
  201.9 3.4 %collective-permute-start.14 = (f32[256,256]{1,0:T(8,128)S(1)}, f32[256,256]{1,0:T(8,128)S(1)}, u32[]{:S(2)}, u32[]{:S(2)}) collective-permute-start(f32[256,256]{1,0:T(8,128)S(1)} %get-tuple-element.23), channel_id=1, source_target_pairs={{4,0},{8,4},{12,8},{16,12},{20,16},{24,20},{28,24},{5,1},{9,5},{13... | collective-permute-start | bytes 786440 | tf_op jit(solution)/shard_map/ppermute | solution.py:17
  203.3 11.2 %collective-permute-start.15 = (f32[2,256,128]{2,1,0:T(8,128)S(1)}, f32[2,256,128]{2,1,0:T(8,128)S(1)}, u32[]{:S(2)}, u32[]{:S(2)}) collective-permute-start(f32[2,256,128]{2,1,0:T(8,128)S(1)} %slice.219), channel_id=1, source_target_pairs={{1,0},{2,1},{3,2},{5,4},{6,5},{7,6},{9,8},{10,9},{11,10},{13,12},{... | collective-permute-start | bytes 786440 | tf_op jit(solution)/shard_map/ppermute | solution.py:17
where the time goes:
time: 218 us; the launch traced here: 216 us
  waiting for transfers between devices  76.9 us (35%)
  starting transfers between devices  44.2 us (20%)
  local copies, waits for them, and re-layouts  43.4 us (20%)
  matrix products  28.3 us (13%)
  other arithmetic  22 us (10%)
    ppermute x16, waiting for transfers between devices, from_behind(): lax.ppermute(value, axis, [(source, source + steps) for source in range(i...  56.8 us
    ppermute x16, starting transfers between devices, from_behind(): lax.ppermute(value, axis, [(source, source + steps) for source in range(i...  35.2 us
    all_to_all x1, waiting for transfers between devices, shards(): lax.all_to_all(send_tiles, 'gx', split_axis=0, concat_axis=0, tiled=True)  20 us
    dot_general x4, matrix products, shards(): jnp.einsum('ncm,nmk->nck', jnp.concatenate([west_in, east_part, -from_sou...  18.8 us
    gather x3, local copies, waits for them, and re-layouts, arranged(): picked = jnp.take(jnp.take(full_tiles, source, axis=0), source, axis=1)  10.9 us
    dot_general x1, matrix products, shards(): jnp.einsum('jka,jkb->jab', factor_panels[:, 0, 0], factor_panels[:, 0, 1]...  9.54 us
    reshape x1, local copies, waits for them, and re-layouts, arranged(): return picked.transpose(0, 2, 1, 3).reshape(NB * block_len, NB * block_len)  6.94 us
    select_n x1, other arithmetic, tile_form(): return jnp.where(keep_upper, upper_f, flipped)  5.63 us
  transfers between devices with their start and end apart: 18, of which 12 were waited for; matrix products, arithmetic and copies ran while one was open for 10% of the time, Pallas kernels for 0%

commit v1 on v0

v1 whole, which is shorter than its diff:
```python
import functools

import jax
import jax.numpy as jnp
from jax import lax
from jax.experimental import pallas as pl
from jax.experimental.pallas import tpu as pltpu
from jax.sharding import PartitionSpec as P

NB = 6
ITERS = 4
CHEB_LOW = 0.2
CHEB_HIGH = 7.0
MESH = pl.DeviceIdType.MESH
F32 = jnp.float32
BF16 = jnp.bfloat16


def upper_count(blocks):
    return blocks * (blocks + 1) // 2


def kernel(
    gx_n, gy_n, jobs, subs, cap, blk,
    east_ref, panels_ref, rhs_ref, mult_ref, res_ref,
    panels, tiles, send_buf, got, mats, x_ref, r_ref, y_ref, xb_ref,
    rw, re, rs, rn, sw, se, ss, sn, iw, isou,
    first_tile, panel_sem, tile_send, tile_recv, face_send, face_recv, init_send, init_recv,
):
    gx = lax.axis_index("gx")
    gy = lax.axis_index("gy")
    rows = rhs_ref.shape[2]
    two = 2 * blk
    south_n = (gy > 0).astype(jnp.int32)
    north_n = (gy < gy_n - 1).astype(jnp.int32)

    def panel_copy(j):
        return pltpu.make_async_copy(panels_ref.at[j, 0], panels.at[j], panel_sem.at[j])

    for j in range(jobs):
        panel_copy(j).start()

    @pl.when(gx == 0)
    def _():
        rw[...] = jnp.zeros_like(rw)
        iw[...] = jnp.zeros_like(iw)

    @pl.when(gx == gx_n - 1)
    def _():
        re[...] = jnp.zeros_like(re)

    @pl.when(gy == 0)
    def _():
        rs[...] = jnp.zeros_like(rs)
        isou[...] = jnp.zeros_like(isou)

    @pl.when(gy == gy_n - 1)
    def _():
        rn[...] = jnp.zeros_like(rn)

    barrier = pltpu.get_barrier_semaphore()

    @pl.loop(1, gx_n)
    def _(i):
        pl.semaphore_signal(barrier, inc=1, device_id=(lax.rem(gx + i, gx_n), gy), device_id_type=MESH)

    @pl.when(gy > 0)
    def _():
        pl.semaphore_signal(barrier, inc=1, device_id=(gx, gy - 1), device_id_type=MESH)

    @pl.when(gy < gy_n - 1)
    def _():
        pl.semaphore_signal(barrier, inc=1, device_id=(gx, gy + 1), device_id_type=MESH)

    pl.semaphore_wait(barrier, gx_n - 1 + south_n + north_n)

    def remote(src, dst, send, recv, dgx, dgy):
        return pltpu.make_async_remote_copy(
            src_ref=src, dst_ref=dst, send_sem=send, recv_sem=recv,
            device_id=(dgx, dgy), device_id_type=MESH,
        )

    has_w, has_e, has_s, has_n = gx > 0, gx < gx_n - 1, gy > 0, gy < gy_n - 1
    gxm, gxp = jnp.maximum(gx - 1, 0), jnp.minimum(gx + 1, gx_n - 1)
    gym, gyp = jnp.maximum(gy - 1, 0), jnp.minimum(gy + 1, gy_n - 1)

    init_e = remote(rhs_ref.at[subs - 1, 0, :, pl.ds(0, two)], iw, init_send.at[0], init_recv.at[0], gxp, gy)
    init_n = remote(rhs_ref.at[:, 0, :, pl.ds(two, blk)], isou, init_send.at[1], init_recv.at[1], gx, gyp)
    pl.when(has_e)(lambda: init_e.start())
    pl.when(has_n)(lambda: init_n.start())

    total = jnp.int32(0)
    before = jnp.int32(0)

    def count_step(i, carry):
        total, west = carry
        first_tile[i] = total
        east = east_ref[i, 0]
        return total + upper_count(west + east + south_n + north_n), east

    lax.fori_loop(0, gx_n * subs, count_step, (total, before))

    @pl.loop(0, jobs)
    def _(j):
        panel_copy(j).wait()
        tiles[j] = lax.dot_general(
            panels[j, 0], panels[j, 1], (((0,), (0,)), ((), ())), preferred_element_type=F32
        ).astype(BF16)

    def tile_copy(d, i, src):
        return remote(
            send_buf.at[pl.ds(d * cap, cap)], got.at[pl.ds(src * cap, cap)],
            tile_send.at[i], tile_recv.at[i], d, gy,
        )

    def slot_of(d, q):
        slot = (first_tile[d * subs] + gx_n * q - gx + gx_n - 1) // gx_n
        return jnp.clip(slot, 0, jobs - 1)

    @pl.loop(1, gx_n)
    def _(i):
        d = lax.rem(gx + i, gx_n)
        for q in range(cap):
            send_buf[d * cap + q] = tiles[slot_of(d, q)]
        tile_copy(d, i, gx).start()

    for q in range(cap):
        got[gx * cap + q] = tiles[slot_of(gx, q)]

    lane_w = lax.broadcasted_iota(jnp.int32, (1, two), 1) // blk

    def east_at(i):
        return east_ref[gx * subs + i, 0]

    def west_at(i):
        left = east_ref[jnp.maximum(gx * subs + i - 1, 0), 0]
        return left if i > 0 else jnp.where(gx > 0, left, 0)

    masks = []
    for s in range(subs):
        mask_w = (lane_w < west_at(s)).astype(F32)
        mask_e = (lane_w < east_at(s)).astype(F32)
        mask_s = jnp.zeros((1, blk), F32) + south_n.astype(F32)
        mask_n = jnp.zeros((1, blk), F32) + north_n.astype(F32)
        masks.append((mask_w, mask_e, mask_s, mask_n))
    lanes = ((0, two), (two, two), (2 * two, blk), (2 * two + blk, blk))

    center = (CHEB_HIGH + CHEB_LOW) / 2.0
    radius = (CHEB_HIGH - CHEB_LOW) / 2.0
    ratio = center / radius
    rho = 1.0 / ratio

    pl.when(has_w)(lambda: init_e.wait_recv())
    pl.when(has_s)(lambda: init_n.wait_recv())
    pl.when(has_e)(lambda: init_e.wait_send())
    pl.when(has_n)(lambda: init_n.wait_send())
    step = 64

    @pl.loop(0, rows // step)
    def _(c):
        rr = pl.ds(c * step, step)
        for s in range(subs):
            west = -iw[rr, :] if s == 0 else -rhs_ref[s - 1, 0, rr, 0:two]
            parts = (west, rhs_ref[s, 0, rr, 0:two], -isou[s, rr, :], rhs_ref[s, 0, rr, two:two + blk])
            for g, (lo, width) in enumerate(lanes):
                r = parts[g] * masks[s][g]
                u = r / center
                r_ref[s, rr, lo:lo + width] = r
                x_ref[s, rr, lo:lo + width] = u
                xb_ref[s, rr, lo:lo + width] = u.astype(BF16)
                if g == 1:
                    mult_ref[s, 0, rr, 0:two] = u
                if g == 3:
                    mult_ref[s, 0, rr, two:two + blk] = u

    @pl.loop(1, gx_n)
    def _(i):
        copy = tile_copy(lax.rem(gx + i, gx_n), i, gx)
        copy.wait()

    base = first_tile[gx * subs]
    for s in range(subs):
        west, east = west_at(s), east_at(s)
        nb = west + east + south_n + north_n
        limit = NB - 1
        place = [jnp.int32(0), jnp.int32(1), west, west + 1, west + east, west + east + south_n]
        place = [jnp.minimum(p, limit) for p in place]
        for a in range(NB):
            for b in range(a, NB):
                pa, pb = place[a], place[b]
                k = first_tile[gx * subs + s] + pa * nb - pa * (pa - 1) // 2 + pb - pa
                k = jnp.clip(k, base, base + cap * gx_n - 1)
                tile = got[lax.rem(k, gx_n) * cap + (k - base) // gx_n]
                mats[s, a * blk:(a + 1) * blk, b * blk:(b + 1) * blk] = tile
                if a < b:
                    mats[s, b * blk:(b + 1) * blk, a * blk:(a + 1) * blk] = tile.T

    for t in range(ITERS):
        last = t == ITERS - 1

        def product(s, g):
            lo, width = lanes[g]
            return jnp.dot(xb_ref[s], mats[s, :, lo:lo + width], preferred_element_type=F32)

        to_w = remote(sw.at[t], re.at[t], face_send.at[t, 0], face_recv.at[t, 0], gxm, gy)
        to_e = remote(se.at[t], rw.at[t], face_send.at[t, 1], face_recv.at[t, 1], gxp, gy)
        to_s = remote(ss.at[t], rn.at[t], face_send.at[t, 2], face_recv.at[t, 2], gx, gym)
        to_n = remote(sn.at[t], rs.at[t], face_send.at[t, 3], face_recv.at[t, 3], gx, gyp)
        copies = [(to_s, has_s, has_n), (to_w, has_w, has_e)]
        if not last:
            copies += [(to_n, has_n, has_s), (to_e, has_e, has_w)]

        for s in range(subs):
            y = product(s, 2)
            y_ref[s, :, 2 * two:2 * two + blk] = y
            ss[t, s] = y.astype(BF16)
        pl.when(has_s)(to_s.start)
        for s in range(subs):
            y = product(s, 3)
            y_ref[s, :, 2 * two + blk:] = y
            if not last:
                sn[t, s] = y.astype(BF16)
        if not last:
            pl.when(has_n)(to_n.start)
        y = product(0, 0)
        y_ref[0, :, 0:two] = y
        sw[t] = y.astype(BF16)
        pl.when(has_w)(to_w.start)
        y = product(subs - 1, 1)
        y_ref[subs - 1, :, two:2 * two] = y
        if not last:
            se[t] = y.astype(BF16)
            pl.when(has_e)(to_e.start)
        for s in range(subs):
            if s > 0:
                y_ref[s, :, 0:two] = product(s, 0)
            if s < subs - 1:
                y_ref[s, :, two:2 * two] = product(s, 1)

        for copy, sends, receives in copies:
            pl.when(receives)(copy.wait_recv)
            pl.when(sends)(copy.wait_send)

        rho_next = 1.0 / (2.0 * ratio - rho)
        keep, gain = rho_next * rho, 2.0 * rho_next / radius
        rho = rho_next

        @pl.loop(0, rows // step)
        def _(c):
            rr = pl.ds(c * step, step)
            for s in range(subs):
                for g, (lo, width) in enumerate(lanes):
                    if last and g in (0, 2):
                        continue
                    if g == 0:
                        other = rw[t, rr, :].astype(F32) if s == 0 else y_ref[s - 1, rr, two:2 * two]
                    elif g == 1:
                        other = re[t, rr, :].astype(F32) if s == subs - 1 else y_ref[s + 1, rr, 0:two]
                    elif g == 2:
                        other = rs[t, s, rr, :].astype(F32)
                    else:
                        other = rn[t, s, rr, :].astype(F32)
                    y = y_ref[s, rr, lo:lo + width]
                    r = r_ref[s, rr, lo:lo + width] - (y - other) * masks[s][g]
                    olo, ohi = (0, two) if g == 1 else (two, two + blk)
                    if last:
                        res_ref[s, 0, rr, olo:ohi] = r
                        continue
                    u = keep * x_ref[s, rr, lo:lo + width] + gain * r
                    r_ref[s, rr, lo:lo + width] = r
                    x_ref[s, rr, lo:lo + width] = u
                    xb_ref[s, rr, lo:lo + width] = u.astype(BF16)
                    if g in (1, 3):
                        mult_ref[s, 0, rr, olo:ohi] = mult_ref[s, 0, rr, olo:ohi] + u


def shards(gx_n, gy_n, east_blocks, job_code, factor_panels, dual_rhs):
    jobs = factor_panels.shape[0]
    depth, blk = factor_panels.shape[-2:]
    subs, _, rows, face = dual_rhs.shape
    cap = (subs * upper_count(NB) + gx_n - 1) // gx_n
    width = NB * blk
    vm = pltpu.VMEM
    dma = pltpu.SemaphoreType.DMA
    half = (ITERS, rows, 2 * blk)
    pair = (ITERS, subs, rows, blk)
    out = jax.ShapeDtypeStruct(dual_rhs.shape, F32)
    return pl.pallas_call(
        functools.partial(kernel, gx_n, gy_n, jobs, subs, cap, blk),
        out_shape=(out, out),
        in_specs=[
            pl.BlockSpec(memory_space=pltpu.SMEM),
            pl.BlockSpec(memory_space=pl.ANY),
            pl.BlockSpec(memory_space=vm),
        ],
        out_specs=(pl.BlockSpec(memory_space=vm), pl.BlockSpec(memory_space=vm)),
        scratch_shapes=[
            vm((jobs, 2, depth, blk), BF16),
            vm((jobs, blk, blk), BF16),
            vm((gx_n * cap, blk, blk), BF16),
            vm((gx_n * cap, blk, blk), BF16),
            vm((subs, width, width), BF16),
            vm((subs, rows, width), F32),
            vm((subs, rows, width), F32),
            vm((subs, rows, width), F32),
            vm((subs, rows, width), BF16),
            vm(half, BF16), vm(half, BF16), vm(pair, BF16), vm(pair, BF16),
            vm(half, BF16), vm(half, BF16), vm(pair, BF16), vm(pair, BF16),
            vm((rows, 2 * blk), F32),
            vm((subs, rows, blk), F32),
            pltpu.SMEM((gx_n * subs,), jnp.int32),
            dma((jobs,)), dma((gx_n,)), dma((gx_n,)),
            dma((ITERS, 4)), dma((ITERS, 4)), dma((2,)), dma((2,)),
        ],
        compiler_params=pltpu.CompilerParams(
            collective_id=0, has_side_effects=True, vmem_limit_bytes=56 * 2**20
        ),
    )(east_blocks, factor_panels, dual_rhs)


def solution(mesh):
    in_specs = (
        P(None, "gy"),
        P("gx", "gy"),
        P("gx", "gy", None, None, None),
        P("gx", "gy", None, None),
    )
    out_specs = (P("gx", "gy", None, None), P("gx", "gy", None, None))
    body = functools.partial(shards, mesh.shape["gx"], mesh.shape["gy"])
    return jax.shard_map(body, mesh=mesh, in_specs=in_specs, out_specs=out_specs, check_vma=False)
```

time: 218 us -> 63.3 us (0.29)
  waiting for transfers between devices: 76.9 us -> 0 us
  Pallas kernels: 0 us -> 56.9 us
  starting transfers between devices: 44.2 us -> 0 us
  local copies, waits for them, and re-layouts: 43.4 us -> 5.46 us
  matrix products: 28.3 us -> 0 us
  other arithmetic: 22 us -> 0 us
    pallas_call x0 -> x1, Pallas kernels: none -> 56.9 us  [shards(): pl.pallas_call(functools.partial(kernel, gx_n, gy_n, jobs, subs, cap, blk...]
    ppermute x16 -> x0, waiting for transfers between devices: 56.8 us -> none  [from_behind(): lax.ppermute(value, axis, [(source, source + steps) for source in range(i...]
    ppermute x16 -> x0, starting transfers between devices: 35.2 us -> none  [from_behind(): lax.ppermute(value, axis, [(source, source + steps) for source in range(i...]
    dot_general x5 -> x0, matrix products: 28.3 us -> none  [the longest x4 18.8 us: shards(): jnp.einsum('ncm,nmk->nck', jnp.concatenate([west_in, east_part, -from_sou...]
    all_to_all x2 -> x0, waiting for transfers between devices: 20 us -> none  [the longest x1 20 us: shards(): lax.all_to_all(send_tiles, 'gx', split_axis=0, concat_axis=0, tiled=True)]
    select_n x6 -> x0, other arithmetic: 12.4 us -> none  [the longest x1 5.63 us: tile_form(): return jnp.where(keep_upper, upper_f, flipped)]
    gather x3 -> x0, local copies, waits for them, and re-layouts: 10.9 us -> none  [arranged(): picked = jnp.take(jnp.take(full_tiles, source, axis=0), source, axis=1)]
    scatter x3 -> x0, local copies, waits for them, and re-layouts: 10.1 us -> none  [the longest x1 5.14 us: shards(): upper_tiles = jnp.zeros((sub_count * NB * NB, block_len, block_len), jnp....]
  transfers between devices with their start and end apart: 18 -> 0, of which waited for: 12 -> 0; matrix products, arithmetic and copies ran while one was open for 10% -> 0% of each run, Pallas kernels for 0% -> 0%
where the time goes in v1:
time: 63.3 us; the launch traced here: 63 us
  Pallas kernels  56.9 us (90%)
  local copies, waits for them, and re-layouts  5.46 us (9%)
  between operations  0.64 us (1%)
    pallas_call x1, Pallas kernels, shards(): pl.pallas_call(functools.partial(kernel, gx_n, gy_n, jobs, subs, cap, blk...  56.9 us
    unnamed x3, local copies, waits for them, and re-layouts  5.46 us

profile of v1, /device:TPU:0, one launch (start us, length us, event | category | flops | bytes accessed | tf_op | source)
XLA Modules:
  0.0 63.0 jit_solution(14725503041369308493)
XLA Ops:
  0.6 1.3 %copy.5.east_ref = s32[16,1]{1,0:T(8,128)} copy(s32[16,1]{0,1:T(1,128)} %param.4) | data formatting | bytes 128 | tf_op args[0]
  2.0 56.9 %shard_map.50 = (f32[2,1,256,384]{3,2,1,0:T(8,128)}, f32[2,1,256,384]{3,2,1,0:T(8,128)}) custom-call(s32[16,1]{1,0:T(8,128)} %copy.5.east_ref, bf16[25,1,2,1536,128]{4,3,2,1,0:T(8,128)(2,1)} %panels_ref.1, f32[2,1,256,384]{3,2,1,0:T(8,128)} %rhs_ref.1), custom_call_target="tpu_custom_call" | custom-call | tf_op jit(solution)/shard_map/pallas_call | solution.py:288
  58.9 2.1 %copy.8 = f32[2,1,256,384]{3,2,1,0:T(8,128)} copy(f32[2,1,256,384]{3,2,1,0:T(8,128)} %get-tuple-element.4) | data formatting | bytes 1572864
  61.0 2.1 %copy.9 = f32[2,1,256,384]{3,2,1,0:T(8,128)} copy(f32[2,1,256,384]{3,2,1,0:T(8,128)} %get-tuple-element.5) | data formatting | bytes 1572864

commit v2 on v1

--- a/solution.py
+++ b/solution.py
@@ -9,6 +9,7 @@
 
 NB = 6
 ITERS = 4
+HALVES = 2
 CHEB_LOW = 0.2
 CHEB_HIGH = 7.0
 MESH = pl.DeviceIdType.MESH
@@ -95,10 +96,11 @@
     def count_step(i, carry):
         total, west = carry
         first_tile[i] = total
-        east = east_ref[i, 0]
+        east = east_ref[0, i]
         return total + upper_count(west + east + south_n + north_n), east
 
-    lax.fori_loop(0, gx_n * subs, count_step, (total, before))
+    total, _ = lax.fori_loop(0, gx_n * subs, count_step, (total, before))
+    first_tile[gx_n * subs] = total
 
     @pl.loop(0, jobs)
     def _(j):
@@ -115,7 +117,8 @@
 
     def slot_of(d, q):
         slot = (first_tile[d * subs] + gx_n * q - gx + gx_n - 1) // gx_n
-        return jnp.clip(slot, 0, jobs - 1)
+        final = (first_tile[d * subs + subs] + gx_n - 1 - gx) // gx_n - 1
+        return jnp.clip(jnp.minimum(slot, final), 0, jobs - 1)
 
     @pl.loop(1, gx_n)
     def _(i):
@@ -130,10 +133,10 @@
     lane_w = lax.broadcasted_iota(jnp.int32, (1, two), 1) // blk
 
     def east_at(i):
-        return east_ref[gx * subs + i, 0]
+        return east_ref[0, gx * subs + i]
 
     def west_at(i):
-        left = east_ref[jnp.maximum(gx * subs + i - 1, 0), 0]
+        left = east_ref[0, jnp.maximum(gx * subs + i - 1, 0)]
         return left if i > 0 else jnp.where(gx > 0, left, 0)
 
     masks = []
@@ -178,7 +181,7 @@
         copy = tile_copy(lax.rem(gx + i, gx_n), i, gx)
         copy.wait()
 
-    base = first_tile[gx * subs]
+    base, end = first_tile[gx * subs], first_tile[gx * subs + subs]
     for s in range(subs):
         west, east = west_at(s), east_at(s)
         nb = west + east + south_n + north_n
@@ -189,77 +192,83 @@
             for b in range(a, NB):
                 pa, pb = place[a], place[b]
                 k = first_tile[gx * subs + s] + pa * nb - pa * (pa - 1) // 2 + pb - pa
-                k = jnp.clip(k, base, base + cap * gx_n - 1)
+                k = jnp.clip(k, base, end - 1)
                 tile = got[lax.rem(k, gx_n) * cap + (k - base) // gx_n]
                 mats[s, a * blk:(a + 1) * blk, b * blk:(b + 1) * blk] = tile
                 if a < b:
                     mats[s, b * blk:(b + 1) * blk, a * blk:(a + 1) * blk] = tile.T
 
-    for t in range(ITERS):
+    part = rows // HALVES
+
+    def product(h, s, g):
+        lo, width = lanes[g]
+        return jnp.dot(
+            xb_ref[s, h * part:(h + 1) * part, :], mats[s, :, lo:lo + width], preferred_element_type=F32
+        )
+
+    def halo(t, h):
+        sems = lambda g: (face_send.at[t, h, g], face_recv.at[t, h, g])
+        to_s = remote(ss.at[t, h], rn.at[t, h], *sems(2), gx, gym), has_s, has_n
+        to_w = remote(sw.at[t, h], re.at[t, h], *sems(0), gxm, gy), has_w, has_e
+        if t == ITERS - 1:
+            return to_s, to_w
+        to_n = remote(sn.at[t, h], rs.at[t, h], *sems(3), gx, gyp), has_n, has_s
+        to_e = remote(se.at[t, h], rw.at[t, h], *sems(1), gxp, gy), has_e, has_w
+        return to_s, to_w, to_n, to_e
+
+    def multiply(t, h):
+        copies = halo(t, h)
         last = t == ITERS - 1
-
-        def product(s, g):
-            lo, width = lanes[g]
-            return jnp.dot(xb_ref[s], mats[s, :, lo:lo + width], preferred_element_type=F32)
-
-        to_w = remote(sw.at[t], re.at[t], face_send.at[t, 0], face_recv.at[t, 0], gxm, gy)
-        to_e = remote(se.at[t], rw.at[t], face_send.at[t, 1], face_recv.at[t, 1], gxp, gy)
-        to_s = remote(ss.at[t], rn.at[t], face_send.at[t, 2], face_recv.at[t, 2], gx, gym)
-        to_n = remote(sn.at[t], rs.at[t], face_send.at[t, 3], face_recv.at[t, 3], gx, gyp)
-        copies = [(to_s, has_s, has_n), (to_w, has_w, has_e)]
+        rr = slice(h * part, (h + 1) * part)
+        for s in range(subs):
+            y = product(h, s, 2)
+            y_ref[s, rr, 2 * two:2 * two + blk] = y
+            ss[t, h, s] = y.astype(BF16)
+        pl.when(has_s)(copies[0][0].start)
+        for s in range(subs):
+            y = product(h, s, 3)
+            y_ref[s, rr, 2 * two + blk:] = y
+            if not last:
+                sn[t, h, s] = y.astype(BF16)
         if not last:
-            copies += [(to_n, has_n, has_s), (to_e, has_e, has_w)]
-
-        for s in range(subs):
-            y = product(s, 2)
-            y_ref[s, :, 2 * two:2 * two + blk] = y
-            ss[t, s] = y.astype(BF16)
-        pl.when(has_s)(to_s.start)
-        for s in range(subs):
-            y = product(s, 3)
-            y_ref[s, :, 2 * two + blk:] = y
-            if not last:
-                sn[t, s] = y.astype(BF16)
+            pl.when(has_n)(copies[2][0].start)
+        y = product(h, 0, 0)
+        y_ref[0, rr, 0:two] = y
+        sw[t, h] = y.astype(BF16)
+        pl.when(has_w)(copies[1][0].start)
+        y = product(h, subs - 1, 1)
+        y_ref[subs - 1, rr, two:2 * two] = y
         if not last:
-            pl.when(has_n)(to_n.start)
-        y = product(0, 0)
-        y_ref[0, :, 0:two] = y
-        sw[t] = y.astype(BF16)
-        pl.when(has_w)(to_w.start)
-        y = product(subs - 1, 1)
-        y_ref[subs - 1, :, two:2 * two] = y
-        if not last:
-            se[t] = y.astype(BF16)
-            pl.when(has_e)(to_e.start)
+            se[t, h] = y.astype(BF16)
+            pl.when(has_e)(copies[3][0].start)
         for s in range(subs):
             if s > 0:
-                y_ref[s, :, 0:two] = product(s, 0)
+                y_ref[s, rr, 0:two] = product(h, s, 0)
             if s < subs - 1:
-                y_ref[s, :, two:2 * two] = product(s, 1)
-
-        for copy, sends, receives in copies:
+                y_ref[s, rr, two:2 * two] = product(h, s, 1)
+
+    def advance(t, h, keep, gain):
+        last = t == ITERS - 1
+        for copy, sends, receives in halo(t, h):
             pl.when(receives)(copy.wait_recv)
             pl.when(sends)(copy.wait_send)
 
-        rho_next = 1.0 / (2.0 * ratio - rho)
-        keep, gain = rho_next * rho, 2.0 * rho_next / radius
-        rho = rho_next
-
-        @pl.loop(0, rows // step)
+        @pl.loop(0, part // step)
         def _(c):
-            rr = pl.ds(c * step, step)
+            ll = pl.ds(c * step, step)
+            rr = pl.ds(h * part + c * step, step)
             for s in range(subs):
                 for g, (lo, width) in enumerate(lanes):
                     if last and g in (0, 2):
                         continue
                     if g == 0:
-                        other = rw[t, rr, :].astype(F32) if s == 0 else y_ref[s - 1, rr, two:2 * two]
+                        other = rw[t, h, ll, :].astype(F32) if s == 0 else y_ref[s - 1, rr, two:2 * two]
                     elif g == 1:
-                        other = re[t, rr, :].astype(F32) if s == subs - 1 else y_ref[s + 1, rr, 0:two]
+                        other = re[t, h, ll, :].astype(F32) if s == subs - 1 else y_ref[s + 1, rr, 0:two]
                     elif g == 2:
-                        other = rs[t, s, rr, :].astype(F32)
+                        other = rs[t, h, s, ll, :].astype(F32)
                     else:
-                        other = rn[t, s, rr, :].astype(F32)
+                        other = rn[t, h, s, ll, :].astype(F32)
                     y = y_ref[s, rr, lo:lo + width]
                     r = r_ref[s, rr, lo:lo + width] - (y - other) * masks[s][g]
                     olo, ohi = (0, two) if g == 1 else (two, two + blk)
@@ -273,6 +282,28 @@
                     if g in (1, 3):
                         mult_ref[s, 0, rr, olo:ohi] = mult_ref[s, 0, rr, olo:ohi] + u
 
+    for h in range(HALVES):
+        multiply(0, h)
+    for t in range(ITERS):
+        rho_next = 1.0 / (2.0 * ratio - rho)
+        keep, gain = rho_next * rho, 2.0 * rho_next / radius
+        rho = rho_next
+        for h in range(HALVES):
+            advance(t, h, keep, gain)
+            if t < ITERS - 1:
+                multiply(t + 1, h)
+
+
+def finish(mult_in, res_in, mult_out, res_out, sems):
+    copies = [
+        pltpu.make_async_copy(mult_in, mult_out, sems.at[0]),
+        pltpu.make_async_copy(res_in, res_out, sems.at[1]),
+    ]
+    for copy in copies:
+        copy.start()
+    for copy in copies:
+        copy.wait()
+
 
 def shards(gx_n, gy_n, east_blocks, job_code, factor_panels, dual_rhs):
     jobs = factor_panels.shape[0]
@@ -282,10 +313,10 @@
     width = NB * blk
     vm = pltpu.VMEM
     dma = pltpu.SemaphoreType.DMA
-    half = (ITERS, rows, 2 * blk)
-    pair = (ITERS, subs, rows, blk)
+    half = (ITERS, HALVES, rows // HALVES, 2 * blk)
+    pair = (ITERS, HALVES, subs, rows // HALVES, blk)
     out = jax.ShapeDtypeStruct(dual_rhs.shape, F32)
-    return pl.pallas_call(
+    mult, res = pl.pallas_call(
         functools.partial(kernel, gx_n, gy_n, jobs, subs, cap, blk),
         out_shape=(out, out),
         in_specs=[
@@ -308,14 +339,22 @@
             vm(half, BF16), vm(half, BF16), vm(pair, BF16), vm(pair, BF16),
             vm((rows, 2 * blk), F32),
             vm((subs, rows, blk), F32),
-            pltpu.SMEM((gx_n * subs,), jnp.int32),
+            pltpu.SMEM((gx_n * subs + 1,), jnp.int32),
             dma((jobs,)), dma((gx_n,)), dma((gx_n,)),
-            dma((ITERS, 4)), dma((ITERS, 4)), dma((2,)), dma((2,)),
+            dma((ITERS, HALVES, 4)), dma((ITERS, HALVES, 4)), dma((2,)), dma((2,)),
         ],
         compiler_params=pltpu.CompilerParams(
             collective_id=0, has_side_effects=True, vmem_limit_bytes=56 * 2**20
         ),
-    )(east_blocks, factor_panels, dual_rhs)
+    )(east_blocks.T, factor_panels, dual_rhs)
+    anywhere = pl.BlockSpec(memory_space=pl.ANY)
+    return pl.pallas_call(
+        finish,
+        out_shape=(out, out),
+        in_specs=[anywhere, anywhere],
+        out_specs=(anywhere, anywhere),
+        scratch_shapes=[dma((2,))],
+    )(mult, res)
 
 
 def solution(mesh):

time: 63.3 us -> 102 us (1.61)
  Pallas kernels: 56.9 us -> 101 us
  local copies, waits for them, and re-layouts: 5.46 us -> 0 us
    pallas_call x0 -> x1, Pallas kernels: none -> 48.8 us  [shards(): pl.pallas_call(finish, out_shape=(out, out), in_specs=[anywhere, anywhere...]
    unnamed x3 -> x0, local copies, waits for them, and re-layouts: 5.46 us -> none
    pallas_call x1, Pallas kernels: 56.9 us -> 52.7 us  [shards(): pl.pallas_call(functools.partial(kernel, gx_n, gy_n, jobs, subs, cap, blk...]
where the time goes in v2:
time: 102 us
  Pallas kernels  101 us (99%)
    pallas_call x1, Pallas kernels, shards(): pl.pallas_call(functools.partial(kernel, gx_n, gy_n, jobs, subs, cap, blk...  52.7 us
    pallas_call x1, Pallas kernels, shards(): pl.pallas_call(finish, out_shape=(out, out), in_specs=[anywhere, anywhere...  48.8 us

profile of v2, /device:TPU:0, one launch (start us, length us, event | category | flops | bytes accessed | tf_op | source)
XLA Modules:
  0.0 102.1 jit_solution(14516356304840689496)
XLA Ops:
  0.6 52.7 %shard_map.50 = (f32[2,1,256,384]{3,2,1,0:T(8,128)}, f32[2,1,256,384]{3,2,1,0:T(8,128)}) custom-call(s32[1,16]{1,0:T(1,128)} %bitcast.1, bf16[25,1,2,1536,128]{4,3,2,1,0:T(8,128)(2,1)} %panels_ref.1, f32[2,1,256,384]{3,2,1,0:T(8,128)} %rhs_ref.1), custom_call_target="tpu_custom_call" | custom-call | tf_op jit(solution)/shard_map/pallas_call | solution.py:319
  53.3 48.8 %shard_map.51 = (f32[2,1,256,384]{3,2,1,0:T(8,128)}, f32[2,1,256,384]{3,2,1,0:T(8,128)}) custom-call(f32[2,1,256,384]{3,2,1,0:T(8,128)} %get-tuple-element.4.mult_in, f32[2,1,256,384]{3,2,1,0:T(8,128)} %get-tuple-element.5.res_in), custom_call_target="tpu_custom_call" | custom-call | tf_op jit(solution)/shard_map/pallas_call | solution.py:351

commit v3 on v2

--- a/solution.py
+++ b/solution.py
@@ -294,17 +294,6 @@
                 multiply(t + 1, h)
 
 
-def finish(mult_in, res_in, mult_out, res_out, sems):
-    copies = [
-        pltpu.make_async_copy(mult_in, mult_out, sems.at[0]),
-        pltpu.make_async_copy(res_in, res_out, sems.at[1]),
-    ]
-    for copy in copies:
-        copy.start()
-    for copy in copies:
-        copy.wait()
-
-
 def shards(gx_n, gy_n, east_blocks, job_code, factor_panels, dual_rhs):
     jobs = factor_panels.shape[0]
     depth, blk = factor_panels.shape[-2:]
@@ -316,7 +305,7 @@
     half = (ITERS, HALVES, rows // HALVES, 2 * blk)
     pair = (ITERS, HALVES, subs, rows // HALVES, blk)
     out = jax.ShapeDtypeStruct(dual_rhs.shape, F32)
-    mult, res = pl.pallas_call(
+    return pl.pallas_call(
         functools.partial(kernel, gx_n, gy_n, jobs, subs, cap, blk),
         out_shape=(out, out),
         in_specs=[
@@ -347,14 +336,6 @@
             collective_id=0, has_side_effects=True, vmem_limit_bytes=56 * 2**20
         ),
     )(east_blocks.T, factor_panels, dual_rhs)
-    anywhere = pl.BlockSpec(memory_space=pl.ANY)
-    return pl.pallas_call(
-        finish,
-        out_shape=(out, out),
-        in_specs=[anywhere, anywhere],
-        out_specs=(anywhere, anywhere),
-        scratch_shapes=[dma((2,))],
-    )(mult, res)
 
 
 def solution(mesh):

time: 102 us -> 57.7 us (0.57)
  Pallas kernels: 101 us -> 52.7 us
  local copies, waits for them, and re-layouts: 0 us -> 4.13 us
    pallas_call x1 -> x0, Pallas kernels: 48.8 us -> none  [shards(): pl.pallas_call(finish, out_shape=(out, out), in_specs=[anywhere, anywhere...]
    unnamed x0 -> x2, local copies, waits for them, and re-layouts: none -> 4.13 us
where the time goes in v3:
time: 57.7 us; the launch traced here: 57.4 us
  Pallas kernels  52.7 us (91%)
  local copies, waits for them, and re-layouts  4.13 us (7%)
  between operations  0.64 us (1%)
    pallas_call x1, Pallas kernels, shards(): pl.pallas_call(functools.partial(kernel, gx_n, gy_n, jobs, subs, cap, blk...  52.7 us
    unnamed x2, local copies, waits for them, and re-layouts  4.13 us

profile of v3, /device:TPU:0, one launch (start us, length us, event | category | flops | bytes accessed | tf_op | source)
XLA Modules:
  0.0 57.4 jit_solution(7456054567737502825)
XLA Ops:
  0.6 52.7 %shard_map.50 = (f32[2,1,256,384]{3,2,1,0:T(8,128)}, f32[2,1,256,384]{3,2,1,0:T(8,128)}) custom-call(s32[1,16]{1,0:T(1,128)} %bitcast.1, bf16[25,1,2,1536,128]{4,3,2,1,0:T(8,128)(2,1)} %panels_ref.1, f32[2,1,256,384]{3,2,1,0:T(8,128)} %rhs_ref.1), custom_call_target="tpu_custom_call" | custom-call | tf_op jit(solution)/shard_map/pallas_call | solution.py:308
  53.3 2.1 %copy.7 = f32[2,1,256,384]{3,2,1,0:T(8,128)} copy(f32[2,1,256,384]{3,2,1,0:T(8,128)} %get-tuple-element.4) | data formatting | bytes 1572864
  55.4 2.1 %copy.8 = f32[2,1,256,384]{3,2,1,0:T(8,128)} copy(f32[2,1,256,384]{3,2,1,0:T(8,128)} %get-tuple-element.5) | data formatting | bytes 1572864
